TPU v7x, 32 devices: a whole 2x2x4 slice. The times are simulated.
32 devices in a mesh: clips: 2 (over x), segment: 2 (over core), rows: 8 (over z, y).
Axes of the slice: x: 2, y: 2, z: 4, core: 2. Of those that a mesh axis runs over, the one named last changes fastest.
Arguments:
- latent: float32 [4, 48, 512], P('clips', 'rows', 'segment'), parts along dimension 0, may hold values from -6 to 6
- stale: bfloat16 [2, 4, 48, 128, 320], P('segment', 'clips', 'rows'), parts along dimension 1, may hold values from -6 to 6
- timesteps: int32 [4], P('clips'), parts along dimension 0, may hold values from 0 to 999
- w_in: bfloat16 [4, 320], replicated, may hold values from -3 to 3
- w_enc: bfloat16 [3, 3, 320, 320], replicated, may hold values from -0.109375 to 0.109375
- w_down: bfloat16 [3, 3, 320, 640], replicated, may hold values from -0.109375 to 0.109375
- w_tmid: bfloat16 [3, 640, 640], replicated, may hold values from -0.125 to 0.125
- w_up: bfloat16 [640, 320], replicated, may hold values from -0.25 to 0.25
- w_skip: bfloat16 [640, 320], replicated, may hold values from -0.25 to 0.25
- w_dec: bfloat16 [3, 3, 320, 320], replicated, may hold values from -0.109375 to 0.109375
- w_out: bfloat16 [3, 3, 320, 4], replicated, may hold values from -0.109375 to 0.109375
- w_time: bfloat16 [320, 1280], replicated, may hold values from -0.3125 to 0.3125
Outputs:
- next_latent: float32 [4, 48, 512], P('clips', 'rows', 'segment'), parts along dimension 0
- features: bfloat16 [2, 4, 48, 128, 320], P('segment', 'clips', 'rows'), parts along dimension 1
There are 2 independent parts, one for each index of `clips`. A program takes and returns all parts, laid end to end along the dimension named above; an argument that names none is the same for every part. Nothing has to cross between parts.
Inputs may be any that keep to these rules, and one draw needn't show every extreme that they name: `timesteps`: one diffusion timestep index a step.
All inputs are finite; a program needn't handle non-finite values.
Results may differ from a plain program's by a relative error of at most 0.006.
Values may be sent and summed in bfloat16 or wider, within the bound.
A program may use at most 128 MiB of HBM per device.

v0:
```python
import math

import jax
import jax.numpy as jnp
from jax import lax
from jax.sharding import PartitionSpec as P

EPSILON = 1e-06


def with_halo(value, sides, width):
    for axis, dim in sides:
        size, length = (lax.axis_size(axis), value.shape[dim])
        up = [(i, (i + 1) % size) for i in range(size - 1)]
        down = [(j, i) for i, j in up]
        last = lax.slice_in_dim(value, length - width, length, axis=dim)
        first = lax.slice_in_dim(value, 0, width, axis=dim)
        before = lax.ppermute(last, axis, up)
        after = lax.ppermute(first, axis, down)
        value = jnp.concatenate([before, value, after], axis=dim)
    return value


def swapped(value, axis, stride):
    mask = 2**stride
    pairs = [(source, source ^ mask) for source in range(lax.axis_size(axis))]
    return lax.ppermute(value, axis, pairs)


def from_behind(value, axis, by):
    length = lax.axis_size(axis)
    pairs = [(i, i + by) for i in range(length) if 0 <= i + by < length]
    return lax.ppermute(value, axis, pairs)


def normed(values):
    scale = lax.rsqrt(jnp.mean(values * values, axis=-1, keepdims=True) + EPSILON)
    return jax.nn.silu(values * scale)


def conv_rows(extended, weight, count):
    padded = jnp.pad(extended, ((0, 0), (0, 0), (1, 1), (0, 0)))
    columns = extended.shape[2]
    total = jnp.zeros((extended.shape[0], count, columns, weight.shape[3]), jnp.float32)
    for row_off in range(3):
        for col_off in range(3):
            window = padded[:, row_off : row_off + count, col_off : col_off + columns, :]
            total = total + jnp.einsum(
                "fhwc,co->fhwo",
                window,
                weight[row_off, col_off],
                preferred_element_type=jnp.float32,
            )
    return total


def conv_down(extended, weight, count):
    padded = jnp.pad(extended, ((0, 0), (0, 0), (1, 1), (0, 0)))
    columns = extended.shape[2] // 2
    total = jnp.zeros((extended.shape[0], count, columns, weight.shape[3]), jnp.float32)
    for row_off in range(3):
        for col_off in range(3):
            window = padded[
                :, row_off : row_off + 2 * count : 2, col_off : col_off + 2 * columns : 2, :
            ]
            total = total + jnp.einsum(
                "fhwc,co->fhwo",
                window,
                weight[row_off, col_off],
                preferred_element_type=jnp.float32,
            )
    return total


def temporal(values, weight):
    frames = values.shape[0]
    padded = jnp.pad(values, ((1, 1), (0, 0), (0, 0), (0, 0)))
    total = jnp.zeros(values.shape[:3] + (weight.shape[2],), jnp.float32)
    for offset in range(3):
        total = total + jnp.einsum(
            "fhwc,co->fhwo",
            padded[offset : offset + frames],
            weight[offset],
            preferred_element_type=jnp.float32,
        )
    return total


def time_bias(step_time, w_time):
    half = w_time.shape[0] // 2
    freqs = jnp.exp(-math.log(10000.0) * jnp.arange(half).astype(jnp.float32) / half)
    angles = step_time.astype(jnp.float32) * freqs
    embedded = jnp.concatenate([jnp.sin(angles), jnp.cos(angles)])
    gated = jax.nn.silu(embedded).astype(jnp.bfloat16)
    return jnp.dot(gated[None, :], w_time, preferred_element_type=jnp.float32)[0]


def skip_mix(mid_map, enc_map, w_skip):
    joined = jnp.concatenate([mid_map, enc_map], axis=-1)
    mixed = jnp.einsum("fhwc,co->fhwo", joined, w_skip, preferred_element_type=jnp.float32)
    return (mixed, normed(mixed).astype(jnp.bfloat16))


def body(latent, stale, timesteps, w_in, w_enc, w_down, w_tmid, w_up, w_skip, w_dec, w_out, w_time):
    first = lax.axis_index("segment") == 0
    state = stale[0]
    frames, rows_dev, columns, chans = state.shape
    mid_chans = w_down.shape[3]
    lat_chans = w_in.shape[0]
    half_cols = latent.shape[2]
    current = lax.all_gather(latent, "segment", axis=2, tiled=True)

    def rims(values):
        return with_halo(values, (("rows", 1),), 1)

    for step in range(timesteps.shape[0]):
        other = swapped(state, "segment", 0)
        biases = time_bias(timesteps[step], w_time)
        bias_enc = biases[:chans]
        bias_mid = biases[chans : chans + mid_chans]
        bias_dec = biases[chans + mid_chans :]
        inputs = current.reshape(frames, rows_dev, columns, lat_chans).astype(jnp.bfloat16)

        def enc_front(operands):
            inputs_here, state_here, other_here = operands
            lifted = jnp.einsum(
                "fhwc,co->fhwo", inputs_here, w_in, preferred_element_type=jnp.float32
            )
            return (normed(lifted).astype(jnp.bfloat16), lifted)

        def mid_front(operands):
            inputs_here, state_here, other_here = operands
            gated_enc = normed(other_here.astype(jnp.float32)).astype(jnp.bfloat16)
            return (gated_enc, jnp.zeros(state_here.shape, jnp.float32))

        activated, lifted = lax.cond(first, enc_front, mid_front, (inputs, state, other))
        spread = rims(activated)

        def enc_middle(operands):
            spread_here, lifted_here, state_here, other_here = operands
            fresh = (lifted_here + conv_rows(spread_here, w_enc, rows_dev) + bias_enc).astype(
                jnp.bfloat16
            )
            mixed, gated = skip_mix(other_here, state_here, w_skip)
            return (fresh, mixed, gated)

        def mid_middle(operands):
            spread_here, lifted_here, state_here, other_here = operands
            lowered = conv_down(spread_here, w_down, rows_dev // 2) + bias_mid
            mixed_time = lowered + temporal(normed(lowered).astype(jnp.bfloat16), w_tmid)
            raised = jnp.einsum(
                "fhwc,co->fhwo",
                mixed_time.astype(jnp.bfloat16),
                w_up,
                preferred_element_type=jnp.float32,
            ).astype(jnp.bfloat16)
            fresh = jnp.repeat(jnp.repeat(raised, 2, axis=1), 2, axis=2)
            mixed = jnp.zeros(state_here.shape, jnp.float32)
            gated = jnp.zeros(state_here.shape, jnp.bfloat16)
            return (fresh, mixed, gated)

        fresh, mixed, gated = lax.cond(
            first, enc_middle, mid_middle, (spread, lifted, state, other)
        )
        sheared = rims(gated)

        def enc_tail(operands):
            sheared_here, mixed_here = operands
            decoded = mixed_here + conv_rows(sheared_here, w_dec, rows_dev) + bias_dec
            return normed(decoded).astype(jnp.bfloat16)

        def mid_tail(operands):
            sheared_here, mixed_here = operands
            return jnp.zeros(mixed_here.shape, jnp.bfloat16)

        outlet = lax.cond(first, enc_tail, mid_tail, (sheared, mixed))
        widened = rims(outlet)
        noise = conv_rows(widened, w_out, rows_dev)
        coefficient = (timesteps[step].astype(jnp.float32) + 1.0) / 1000.0
        current = current - coefficient * noise.reshape(frames, rows_dev, columns * lat_chans)
        state = fresh
    spare = from_behind(current[:, :, half_cols:], "segment", 1)
    result = jnp.where(first, current[:, :, :half_cols], spare)
    return (result, state[None])


def solution(mesh):
    placed = (
        P("clips", "rows", "segment"),
        P("segment", "clips", "rows", None, None),
        P("clips"),
        P(),
        P(),
        P(),
        P(),
        P(),
        P(),
        P(),
        P(),
        P(),
    )
    return jax.shard_map(
        body,
        mesh=mesh,
        in_specs=placed,
        out_specs=(P("clips", "rows", "segment"), P("segment", "clips", "rows", None, None)),
        check_vma=False,
    )
```

profile of v0, /device:TPU:0, one launch (start us, length us, event | category | flops | bytes accessed | tf_op | source)
XLA Modules:
  0.0 245.4 jit_solution(10601966086027622090)
XLA Ops:
  5.4 5.4 %conditional.16 = (bf16[2,6,128,320]{2,3,1,0:T(8,128)(2,1)S(1)}, f32[2,6,128,320]{2,3,1,0:T(8,128)}) conditional(s32[]{:T(128)} %convert_element_type.116, bf16[2,6,128,320]{2,3,1,0:T(8,128)(2,1)} %collective-permute-done, (f32[2,6,512]{2,0,1:T(2,128)S(1)}, bf16[4,320]{1,0:T(4,128)(2,1)}) %tuple.61), branch_computations={%region_0.2_spmd, %region_2.4_spmd} | conditional | flops 7872000 | bytes 5016080
  10.9 4.6 %collective-permute-start.1 = (bf16[2,1,128,320]{2,3,1,0:T(8,128)(2,1)S(1)}, bf16[2,1,128,320]{2,3,1,0:T(8,128)(2,1)S(1)}, u32[]{:S(2)}, u32[]{:S(2)}) collective-permute-start(bf16[2,1,128,320]{2,3,1,0:T(8,128)(2,1)S(1)} %get-tuple-element.307), channel_id=1, source_target_pairs={{0,1},{1,2},{2,3},{3,4},{4,5},{5,6},{6,7},{8,9},{9,10},{10,11},{11... | collective-permute-start | bytes 491528 | tf_op jit(solution)/shard_map/ppermute | solution.py:18
  22.9 39.1 %conditional.17 = (bf16[2,6,128,320]{3,0,2,1:T(2,128)(2,1)S(1)}, f32[2,6,128,320]{3,2,1,0:T(8,128)}, bf16[2,6,128,320]{3,2,1,0:T(8,128)(2,1)}, bf16[2,6,128,320]{2,3,1,0:T(8,128)(2,1)}) conditional(s32[]{:T(128)} %convert_element_type.116, (bf16[2,8,128,320]{2,3,1,0:T(8,128)(2,1)S(1)}, bf16[3,3,320,640]{3,2,1,0:T(8,128)(2,1)}, f32[1280]{0:T(1024)S(1)}, ...), branch_computations={%region_4.6_spmd, %region_6.8_spmd} | conditional | flops 3473573376 | bytes 85471832 | solution.py:162
  30.3 4.2 %copy.85 = bf16[3,3,320,320]{2,3,1,0:T(8,128)(2,1)} copy(bf16[3,3,320,320]{3,2,1,0:T(8,128)(2,1)} %get-tuple-element.251) | data formatting | bytes 3686400 | tf_op jit(solution)/shard_map
  41.6 4.1 %add_convert_fusion = bf16[2,6,128,320]{2,3,1,0:T(8,128)(2,1)} fusion(f32[2,6,128,320]{2,3,1,0:T(8,128)} %get-tuple-element.104, f32[2,6,128,320]{2,3,1,0:T(8,128)S(1)} %fusion.52, f32[2,6,128,320]{2,3,1,0:T(8,128)S(1)} %fusion.51, f32[2,6,128,320]{2,3,1,0:T(8,128)S(1)} %fusion.50, f32[2,6,128,320]{2,3,1,0:T(8,128)S(1)} %fusion.54, ...), kind=kOutput, calls=%fused_computation.72 | convolution fusion | flops 319979520 | bytes 20236288 | tf_op jit(solution)/shard_map/cond/branch_1_fun/fhwc,co->fhwo/dot_general | solution.py:48
  63.7 4.3 %collective-permute-start.3 = (bf16[2,1,128,320]{2,3,1,0:T(8,128)(2,1)S(1)}, bf16[2,1,128,320]{2,3,1,0:T(8,128)(2,1)S(1)}, u32[]{:S(2)}, u32[]{:S(2)}) collective-permute-start(bf16[2,1,128,320]{2,3,1,0:T(8,128)(2,1)S(1)} %get-tuple-element.305), channel_id=1, source_target_pairs={{0,1},{1,2},{2,3},{3,4},{4,5},{5,6},{6,7},{8,9},{9,10},{10,11},{11... | collective-permute-start | bytes 491528 | tf_op jit(solution)/shard_map/ppermute | solution.py:18
  70.0 11.4 %collective-permute-start.7 = (bf16[2,6,128,320]{2,3,1,0:T(8,128)(2,1)}, bf16[2,6,128,320]{2,3,1,0:T(8,128)(2,1)}, u32[]{:S(2)}, u32[]{:S(2)}) collective-permute-start(bf16[2,6,128,320]{2,3,1,0:T(8,128)(2,1)} %get-tuple-element.279), channel_id=1, source_target_pairs={{0,8},{8,0},{1,9},{9,1},{2,10},{10,2},{3,11},{11,3},{4,12},{12,4},... | collective-permute-start | bytes 2949128 | tf_op jit(solution)/shard_map/ppermute | solution.py:27
  83.0 33.3 %conditional.18 = (bf16[2,6,128,320]{2,3,1,0:T(8,128)(2,1)S(1)}) conditional(s32[]{:T(128)} %convert_element_type.116, () %tuple.60, (bf16[2,8,128,320]{2,3,1,0:T(8,128)(2,1)S(1)}, bf16[3,3,320,320]{3,2,1,0:T(8,128)(2,1)}, f32[2,6,128,320]{3,2,1,0:T(8,128)}, f32[1280]{0:T(1024)S(1)}) %tuple.64), branch_computations={%region_8.9_spmd, %region_9.11_spmd} | conditional | flops 2840004096 | bytes 66383652 | solution.py:176
  83.4 4.2 %copy.91 = bf16[3,3,320,320]{2,3,1,0:T(8,128)(2,1)} copy(bf16[3,3,320,320]{3,2,1,0:T(8,128)(2,1)} %get-tuple-element.258) | data formatting | bytes 3686400 | tf_op jit(solution)/shard_map
  108.1 7.6 %multiply_reduce_fusion.3 = (f32[2,6,128]{2,1,0:T(8,128)S(1)}, f32[2,6,128,320]{2,3,1,0:T(8,128)S(1)}) fusion(f32[320]{0:T(512)S(1)} %slice.436, f32[2,6,128,320]{2,3,1,0:T(8,128)} %copy.92, bf16[2,8,128,320]{2,3,1,0:T(8,128)(2,1)S(1)} %get-tuple-element.112, bf16[3,3,320,320]{2,3,1,0:T(8,128)(2,1)} %copy.91, f32[2,6,128,320]{2,3,1,0:T(8,128)} %fusion.71, ...), kind=kOutput, calls=%fused_computation.109 | convolution fusion | flops 320469504 | bytes 21224704 | tf_op jit(solution)/shard_map/cond/branch_1_fun/fhwc,co->fhwo/dot_general | solution.py:48
  116.3 6.0 %collective-permute-start.5 = (bf16[2,1,128,320]{2,3,1,0:T(8,128)(2,1)S(1)}, bf16[2,1,128,320]{2,3,1,0:T(8,128)(2,1)S(1)}, u32[]{:S(2)}, u32[]{:S(2)}) collective-permute-start(bf16[2,1,128,320]{2,3,1,0:T(8,128)(2,1)S(1)} %get-tuple-element.303), channel_id=1, source_target_pairs={{0,1},{1,2},{2,3},{3,4},{4,5},{5,6},{6,7},{8,9},{9,10},{10,11},{11... | collective-permute-start | bytes 491528 | tf_op jit(solution)/shard_map/ppermute | solution.py:18
  125.1 5.0 %collective-permute-done.6 = bf16[2,1,128,320]{2,3,1,0:T(8,128)(2,1)S(1)} collective-permute-done((bf16[2,1,128,320]{2,3,1,0:T(8,128)(2,1)S(1)}, bf16[2,1,128,320]{2,3,1,0:T(8,128)(2,1)S(1)}, u32[]{:S(2)}, u32[]{:S(2)}) %collective-permute-start.6) | collective-permute-done | bytes 163872 | tf_op jit(solution)/shard_map/ppermute | solution.py:19
  135.3 4.9 %conditional.19 = (bf16[2,6,128,320]{2,3,1,0:T(8,128)(2,1)S(1)}, f32[2,6,128,320]{2,3,1,0:T(8,128)}) conditional(s32[]{:T(128)} %convert_element_type.116, bf16[2,6,128,320]{2,3,1,0:T(8,128)(2,1)} %collective-permute-done.7, (f32[2,6,512]{2,0,1:T(2,128)S(1)}, bf16[4,320]{1,0:T(4,128)(2,1)S(1)}) %tuple.134), branch_computations={%region_11.13_spmd, %region_13.15_spmd} | conditional | flops 7872000 | bytes 5016080
  140.3 4.8 %collective-permute-start.8 = (bf16[2,1,128,320]{2,3,1,0:T(8,128)(2,1)S(1)}, bf16[2,1,128,320]{2,3,1,0:T(8,128)(2,1)S(1)}, u32[]{:S(2)}, u32[]{:S(2)}) collective-permute-start(bf16[2,1,128,320]{2,3,1,0:T(8,128)(2,1)S(1)} %get-tuple-element.301), channel_id=1, source_target_pairs={{0,1},{1,2},{2,3},{3,4},{4,5},{5,6},{6,7},{8,9},{9,10},{10,11},{11... | collective-permute-start | bytes 491528 | tf_op jit(solution)/shard_map/ppermute | solution.py:18
  147.9 4.4 %collective-permute-done.9 = bf16[2,1,128,320]{2,3,1,0:T(8,128)(2,1)S(1)} collective-permute-done((bf16[2,1,128,320]{2,3,1,0:T(8,128)(2,1)S(1)}, bf16[2,1,128,320]{2,3,1,0:T(8,128)(2,1)S(1)}, u32[]{:S(2)}, u32[]{:S(2)}) %collective-permute-start.9) | collective-permute-done | bytes 163872 | tf_op jit(solution)/shard_map/ppermute | solution.py:19
  153.7 26.2 %conditional.20 = (f32[2,6,128,320]{3,2,1,0:T(8,128)}, bf16[2,6,128,320]{3,2,1,0:T(8,128)(2,1)}, bf16[1,2,6,128,320]{3,4,2,1,0:T(8,128)(2,1)}) conditional(s32[]{:T(128)} %convert_element_type.116, (bf16[2,8,128,320]{2,3,1,0:T(8,128)(2,1)S(1)}, bf16[3,3,320,640]{3,2,1,0:T(8,128)(2,1)}, f32[1280]{0:T(1024)S(1)}, bf16[3,640,640]{2,1,0:T(8,128)(2,1)}, ...), branch_computations={%region_15.17_spmd, %region_17.19_spmd} | conditional | flops 3473573376 | bytes 81212008 | solution.py:162
  153.9 4.2 %copy.98 = bf16[3,3,320,320]{2,3,1,0:T(8,128)(2,1)} copy(bf16[3,3,320,320]{3,2,1,0:T(8,128)(2,1)} %get-tuple-element.270) | data formatting | bytes 3686400 | tf_op jit(solution)/shard_map
  165.2 4.1 %fusion.130 = bf16[1,2,6,128,320]{3,4,2,1,0:T(8,128)(2,1)} fusion(f32[2,6,128,320]{2,3,1,0:T(8,128)} %get-tuple-element.125, f32[2,6,128,320]{2,3,1,0:T(8,128)S(1)} %fusion.136, f32[2,6,128,320]{2,3,1,0:T(8,128)S(1)} %fusion.135, f32[2,6,128,320]{2,3,1,0:T(8,128)S(1)} %fusion.134, f32[2,6,128,320]{2,3,1,0:T(8,128)S(1)} %fusion.138, ...), kind=kOutput, calls=%fused_computation.211 | convolution fusion | flops 319979520 | bytes 20236288 | tf_op jit(solution)/shard_map/cond/branch_1_fun/fhwc,co->fhwo/dot_general | solution.py:48
  187.4 4.4 %collective-permute-done.11 = bf16[2,1,128,320]{2,3,1,0:T(8,128)(2,1)S(1)} collective-permute-done((bf16[2,1,128,320]{2,3,1,0:T(8,128)(2,1)S(1)}, bf16[2,1,128,320]{2,3,1,0:T(8,128)(2,1)S(1)}, u32[]{:S(2)}, u32[]{:S(2)}) %collective-permute-start.11) | collective-permute-done | bytes 163872 | tf_op jit(solution)/shard_map/ppermute | solution.py:19
  192.0 33.2 %conditional.21 = (bf16[2,6,128,320]{2,3,1,0:T(8,128)(2,1)S(1)}) conditional(s32[]{:T(128)} %convert_element_type.116, () %tuple.65, (bf16[2,8,128,320]{2,3,1,0:T(8,128)(2,1)S(1)}, bf16[3,3,320,320]{3,2,1,0:T(8,128)(2,1)}, f32[2,6,128,320]{3,2,1,0:T(8,128)}, f32[1280]{0:T(1024)S(1)}) %tuple.69), branch_computations={%region_19.20_spmd, %region_20.22_spmd} | conditional | flops 2840004096 | bytes 66383652 | solution.py:176
  192.2 4.2 %copy.102 = bf16[3,3,320,320]{2,3,1,0:T(8,128)(2,1)} copy(bf16[3,3,320,320]{3,2,1,0:T(8,128)(2,1)} %get-tuple-element.274) | data formatting | bytes 3686400 | tf_op jit(solution)/shard_map
  217.0 7.6 %multiply_reduce_fusion.7 = (f32[2,6,128]{2,1,0:T(8,128)S(1)}, f32[2,6,128,320]{2,3,1,0:T(8,128)S(1)}) fusion(f32[320]{0:T(512)S(1)} %slice.498, f32[2,6,128,320]{2,3,1,0:T(8,128)} %copy.103, bf16[2,8,128,320]{2,3,1,0:T(8,128)(2,1)S(1)} %get-tuple-element.130, bf16[3,3,320,320]{2,3,1,0:T(8,128)(2,1)} %copy.102, f32[2,6,128,320]{2,3,1,0:T(8,128)} %fusion.155, ...), kind=kOutput, calls=%fused_computation.248 | convolution fusion | flops 320469504 | bytes 21224704 | tf_op jit(solution)/shard_map/cond/branch_1_fun/fhwc,co->fhwo/dot_general | solution.py:48
  225.2 4.8 %collective-permute-start.12 = (bf16[2,1,128,320]{2,3,1,0:T(8,128)(2,1)S(1)}, bf16[2,1,128,320]{2,3,1,0:T(8,128)(2,1)S(1)}, u32[]{:S(2)}, u32[]{:S(2)}) collective-permute-start(bf16[2,1,128,320]{2,3,1,0:T(8,128)(2,1)S(1)} %get-tuple-element.297), channel_id=1, source_target_pairs={{0,1},{1,2},{2,3},{3,4},{4,5},{5,6},{6,7},{8,9},{9,10},{10,11},{11... | collective-permute-start | bytes 491528 | tf_op jit(solution)/shard_map/ppermute | solution.py:18
  232.8 4.4 %collective-permute-done.13 = bf16[2,1,128,320]{2,3,1,0:T(8,128)(2,1)S(1)} collective-permute-done((bf16[2,1,128,320]{2,3,1,0:T(8,128)(2,1)S(1)}, bf16[2,1,128,320]{2,3,1,0:T(8,128)(2,1)S(1)}, u32[]{:S(2)}, u32[]{:S(2)}) %collective-permute-start.13) | collective-permute-done | bytes 163872 | tf_op jit(solution)/shard_map/ppermute | solution.py:19
  (165 shorter events, 139.4 us)
Async XLA Ops:
  0.6 16.2 %copy-start = (bf16[320,1280]{1,0:T(8,128)(2,1)S(1)}, bf16[320,1280]{1,0:T(8,128)(2,1)}, u32[]{:S(2)}) copy-start(bf16[320,1280]{1,0:T(8,128)(2,1)} %param.35) | copy-start | bytes 2457604
  0.6 4.7 %collective-permute-start = (bf16[2,6,128,320]{2,3,1,0:T(8,128)(2,1)}, bf16[2,6,128,320]{2,3,1,0:T(8,128)(2,1)}, u32[]{:S(2)}, u32[]{:S(2)}) collective-permute-start(bf16[2,6,128,320]{2,3,1,0:T(8,128)(2,1)} %bitcast.599), channel_id=1, source_target_pairs={{0,8},{8,0},{1,9},{9,1},{2,10},{10,2},{3,11},{11,3},{4,12},{12,4},... | collective-permute-start | bytes 2949128 | tf_op jit(solution)/shard_map/ppermute | solution.py:27
  10.9 7.8 %collective-permute-start.1 = (bf16[2,1,128,320]{2,3,1,0:T(8,128)(2,1)S(1)}, bf16[2,1,128,320]{2,3,1,0:T(8,128)(2,1)S(1)}, u32[]{:S(2)}, u32[]{:S(2)}) collective-permute-start(bf16[2,1,128,320]{2,3,1,0:T(8,128)(2,1)S(1)} %get-tuple-element.307), channel_id=1, source_target_pairs={{0,1},{1,2},{2,3},{3,4},{4,5},{5,6},{6,7},{8,9},{9,10},{10,11},{11... | collective-permute-start | bytes 491528 | tf_op jit(solution)/shard_map/ppermute | solution.py:18
  15.5 7.3 %collective-permute-start.2 = (bf16[2,1,128,320]{2,3,1,0:T(8,128)(2,1)S(1)}, bf16[2,1,128,320]{2,3,1,0:T(8,128)(2,1)S(1)}, u32[]{:S(2)}, u32[]{:S(2)}) collective-permute-start(bf16[2,1,128,320]{2,3,1,0:T(8,128)(2,1)S(1)} %get-tuple-element.308), channel_id=1, source_target_pairs={{1,0},{2,1},{3,2},{4,3},{5,4},{6,5},{7,6},{9,8},{10,9},{11,10},{12... | collective-permute-start | bytes 491528 | tf_op jit(solution)/shard_map/ppermute | solution.py:19
  63.6 17.8 %copy-start.7 = (bf16[2,6,128,320]{2,3,1,0:T(8,128)(2,1)}, bf16[2,6,128,320]{2,3,1,0:T(8,128)(2,1)S(1)}, u32[]{:S(2)}) copy-start(bf16[2,6,128,320]{2,3,1,0:T(8,128)(2,1)S(1)} %copy.88) | copy-start | bytes 2949124
  63.7 17.8 %collective-permute-start.3 = (bf16[2,1,128,320]{2,3,1,0:T(8,128)(2,1)S(1)}, bf16[2,1,128,320]{2,3,1,0:T(8,128)(2,1)S(1)}, u32[]{:S(2)}, u32[]{:S(2)}) collective-permute-start(bf16[2,1,128,320]{2,3,1,0:T(8,128)(2,1)S(1)} %get-tuple-element.305), channel_id=1, source_target_pairs={{0,1},{1,2},{2,3},{3,4},{4,5},{5,6},{6,7},{8,9},{9,10},{10,11},{11... | collective-permute-start | bytes 491528 | tf_op jit(solution)/shard_map/ppermute | solution.py:18
  68.0 13.4 %collective-permute-start.4 = (bf16[2,1,128,320]{2,3,1,0:T(8,128)(2,1)S(1)}, bf16[2,1,128,320]{2,3,1,0:T(8,128)(2,1)}, u32[]{:S(2)}, u32[]{:S(2)}) collective-permute-start(bf16[2,1,128,320]{2,3,1,0:T(8,128)(2,1)S(1)} %get-tuple-element.306), channel_id=1, source_target_pairs={{1,0},{2,1},{3,2},{4,3},{5,4},{6,5},{7,6},{9,8},{10,9},{11,10},{12... | collective-permute-start | bytes 491528 | tf_op jit(solution)/shard_map/ppermute | solution.py:19
  70.0 65.3 %collective-permute-start.7 = (bf16[2,6,128,320]{2,3,1,0:T(8,128)(2,1)}, bf16[2,6,128,320]{2,3,1,0:T(8,128)(2,1)}, u32[]{:S(2)}, u32[]{:S(2)}) collective-permute-start(bf16[2,6,128,320]{2,3,1,0:T(8,128)(2,1)} %get-tuple-element.279), channel_id=1, source_target_pairs={{0,8},{8,0},{1,9},{9,1},{2,10},{10,2},{3,11},{11,3},{4,12},{12,4},... | collective-permute-start | bytes 2949128 | tf_op jit(solution)/shard_map/ppermute | solution.py:27
  87.6 3.2 %copy-start.2 = (bf16[3,3,320,320]{2,3,1,0:T(8,128)(2,1)S(1)}, bf16[3,3,320,320]{2,3,1,0:T(8,128)(2,1)}, u32[]{:S(2)}) copy-start(bf16[3,3,320,320]{2,3,1,0:T(8,128)(2,1)} %copy.91) | copy-start | bytes 5529604 | tf_op jit(solution)/shard_map/cond
  116.3 8.8 %collective-permute-start.5 = (bf16[2,1,128,320]{2,3,1,0:T(8,128)(2,1)S(1)}, bf16[2,1,128,320]{2,3,1,0:T(8,128)(2,1)S(1)}, u32[]{:S(2)}, u32[]{:S(2)}) collective-permute-start(bf16[2,1,128,320]{2,3,1,0:T(8,128)(2,1)S(1)} %get-tuple-element.303), channel_id=1, source_target_pairs={{0,1},{1,2},{2,3},{3,4},{4,5},{5,6},{6,7},{8,9},{9,10},{10,11},{11... | collective-permute-start | bytes 491528 | tf_op jit(solution)/shard_map/ppermute | solution.py:18
  122.3 7.8 %collective-permute-start.6 = (bf16[2,1,128,320]{2,3,1,0:T(8,128)(2,1)S(1)}, bf16[2,1,128,320]{2,3,1,0:T(8,128)(2,1)S(1)}, u32[]{:S(2)}, u32[]{:S(2)}) collective-permute-start(bf16[2,1,128,320]{2,3,1,0:T(8,128)(2,1)S(1)} %get-tuple-element.304), channel_id=1, source_target_pairs={{1,0},{2,1},{3,2},{4,3},{5,4},{6,5},{7,6},{9,8},{10,9},{11,10},{12... | collective-permute-start | bytes 491528 | tf_op jit(solution)/shard_map/ppermute | solution.py:19
  124.5 7.3 %copy-start.11 = (bf16[3,3,320,4]{2,3,1,0:T(4,128)(2,1)S(1)}, bf16[3,3,320,4]{2,3,1,0:T(4,128)(2,1)}, u32[]{:S(2)}) copy-start(bf16[3,3,320,4]{2,3,1,0:T(4,128)(2,1)} %param.34) | copy-start | bytes 69124
  140.3 7.7 %copy-start.8 = (bf16[2,6,128,320]{2,3,1,0:T(8,128)(2,1)}, bf16[2,6,128,320]{2,3,1,0:T(8,128)(2,1)S(1)}, u32[]{:S(2)}) copy-start(bf16[2,6,128,320]{2,3,1,0:T(8,128)(2,1)S(1)} %get-tuple-element.150) | copy-start | bytes 2949124
  140.3 7.6 %collective-permute-start.8 = (bf16[2,1,128,320]{2,3,1,0:T(8,128)(2,1)S(1)}, bf16[2,1,128,320]{2,3,1,0:T(8,128)(2,1)S(1)}, u32[]{:S(2)}, u32[]{:S(2)}) collective-permute-start(bf16[2,1,128,320]{2,3,1,0:T(8,128)(2,1)S(1)} %get-tuple-element.301), channel_id=1, source_target_pairs={{0,1},{1,2},{2,3},{3,4},{4,5},{5,6},{6,7},{8,9},{9,10},{10,11},{11... | collective-permute-start | bytes 491528 | tf_op jit(solution)/shard_map/ppermute | solution.py:18
  145.1 7.2 %collective-permute-start.9 = (bf16[2,1,128,320]{2,3,1,0:T(8,128)(2,1)S(1)}, bf16[2,1,128,320]{2,3,1,0:T(8,128)(2,1)S(1)}, u32[]{:S(2)}, u32[]{:S(2)}) collective-permute-start(bf16[2,1,128,320]{2,3,1,0:T(8,128)(2,1)S(1)} %get-tuple-element.302), channel_id=1, source_target_pairs={{1,0},{2,1},{3,2},{4,3},{5,4},{6,5},{7,6},{9,8},{10,9},{11,10},{12... | collective-permute-start | bytes 491528 | tf_op jit(solution)/shard_map/ppermute | solution.py:19
  169.3 2.6 %copy-start.17 = (bf16[640,320]{0,1:T(8,128)(2,1)S(1)}, bf16[640,320]{0,1:T(8,128)(2,1)}, u32[]{:S(2)}) copy-start(bf16[640,320]{0,1:T(8,128)(2,1)} %get-tuple-element.124) | copy-start | bytes 1228804 | tf_op jit(solution)/shard_map/cond
  181.6 5.8 %collective-permute-start.10 = (bf16[2,1,128,320]{2,3,1,0:T(8,128)(2,1)S(1)}, bf16[2,1,128,320]{2,3,1,0:T(8,128)(2,1)S(1)}, u32[]{:S(2)}, u32[]{:S(2)}) collective-permute-start(bf16[2,1,128,320]{2,3,1,0:T(8,128)(2,1)S(1)} %get-tuple-element.299), channel_id=1, source_target_pairs={{0,1},{1,2},{2,3},{3,4},{4,5},{5,6},{6,7},{8,9},{9,10},{10,11},{11... | collective-permute-start | bytes 491528 | tf_op jit(solution)/shard_map/ppermute | solution.py:18
  184.6 7.2 %collective-permute-start.11 = (bf16[2,1,128,320]{2,3,1,0:T(8,128)(2,1)S(1)}, bf16[2,1,128,320]{2,3,1,0:T(8,128)(2,1)S(1)}, u32[]{:S(2)}, u32[]{:S(2)}) collective-permute-start(bf16[2,1,128,320]{2,3,1,0:T(8,128)(2,1)S(1)} %get-tuple-element.300), channel_id=1, source_target_pairs={{1,0},{2,1},{3,2},{4,3},{5,4},{6,5},{7,6},{9,8},{10,9},{11,10},{12... | collective-permute-start | bytes 491528 | tf_op jit(solution)/shard_map/ppermute | solution.py:19
  192.0 39.4 %copy-start.12 = (bf16[3,3,320,4]{2,3,1,0:T(4,128)(2,1)S(1)}, bf16[3,3,320,4]{2,3,1,0:T(4,128)(2,1)}, u32[]{:S(2)}) copy-start(bf16[3,3,320,4]{2,3,1,0:T(4,128)(2,1)} %param.34) | copy-start | bytes 69124
  196.4 3.2 %copy-start.3 = (bf16[3,3,320,320]{2,3,1,0:T(8,128)(2,1)S(1)}, bf16[3,3,320,320]{2,3,1,0:T(8,128)(2,1)}, u32[]{:S(2)}) copy-start(bf16[3,3,320,320]{2,3,1,0:T(8,128)(2,1)} %copy.102) | copy-start | bytes 5529604 | tf_op jit(solution)/shard_map/cond
  225.2 7.6 %collective-permute-start.12 = (bf16[2,1,128,320]{2,3,1,0:T(8,128)(2,1)S(1)}, bf16[2,1,128,320]{2,3,1,0:T(8,128)(2,1)S(1)}, u32[]{:S(2)}, u32[]{:S(2)}) collective-permute-start(bf16[2,1,128,320]{2,3,1,0:T(8,128)(2,1)S(1)} %get-tuple-element.297), channel_id=1, source_target_pairs={{0,1},{1,2},{2,3},{3,4},{4,5},{5,6},{6,7},{8,9},{9,10},{10,11},{11... | collective-permute-start | bytes 491528 | tf_op jit(solution)/shard_map/ppermute | solution.py:18
  230.0 7.2 %collective-permute-start.13 = (bf16[2,1,128,320]{2,3,1,0:T(8,128)(2,1)S(1)}, bf16[2,1,128,320]{2,3,1,0:T(8,128)(2,1)S(1)}, u32[]{:S(2)}, u32[]{:S(2)}) collective-permute-start(bf16[2,1,128,320]{2,3,1,0:T(8,128)(2,1)S(1)} %get-tuple-element.298), channel_id=1, source_target_pairs={{1,0},{2,1},{3,2},{4,3},{5,4},{6,5},{7,6},{9,8},{10,9},{11,10},{12... | collective-permute-start | bytes 491528 | tf_op jit(solution)/shard_map/ppermute | solution.py:19
  241.1 4.0 %copy-start.1 = (bf16[320,1280]{1,0:T(8,128)(2,1)S(1)}, bf16[320,1280]{1,0:T(8,128)(2,1)}, u32[]{:S(2)}) copy-start(bf16[320,1280]{1,0:T(8,128)(2,1)} %param.35) | copy-start | bytes 2457604
  242.4 2.1 collective-permute-start.14
  (5 other events, 7.9 us)
where the time goes:
time: 250 us; the launch traced here: 245 us
  matrix products  86.9 us (35%)
  local copies, waits for them, and re-layouts  52.4 us (21%)
  starting transfers between devices  48.5 us (19%)
  waiting for transfers between devices  29.2 us (12%)
  other arithmetic  14.8 us (6%)
  loops' own time  8.88 us (4%)
  between operations  2.59 us (1%)
    dot_general x54, matrix products, conv_rows(): jnp.einsum('fhwc,co->fhwo', window, weight[row_off, col_off], preferred_e...  78.8 us
    another operation x15, local copies, waits for them, and re-layouts  41.7 us
    ppermute x6, starting transfers between devices, with_halo(): before = lax.ppermute(last, axis, up)  27.5 us
    ppermute x6, waiting for transfers between devices, with_halo(): after = lax.ppermute(first, axis, down)  22.3 us
    ppermute x2, starting transfers between devices, swapped(): return lax.ppermute(value, axis, pairs)  12 us
    another operation x2, loops' own time, body(): lax.cond(first, enc_middle, mid_middle, (spread, lifted, state, other))  7.9 us
    ppermute x6, starting transfers between devices, with_halo(): after = lax.ppermute(first, axis, down)  7.75 us
    concatenate x6, other arithmetic, with_halo(): value = jnp.concatenate([before, value, after], axis=dim)  6.62 us
  transfers between devices with their start and end apart: 15, of which 11 were waited for; matrix products, arithmetic and copies ran while one was open for 17% of the time, Pallas kernels for 0%

commit v1 on v0

v1 whole, which is shorter than its diff:
```python
import functools
import math

import jax
import jax.numpy as jnp
from jax import lax
from jax.experimental import pallas as pl
from jax.experimental.pallas import tpu as pltpu
from jax.sharding import PartitionSpec as P

EPSILON = 1e-06
F32 = jnp.float32
BF16 = jnp.bfloat16
MESH = pl.DeviceIdType.MESH
SUB = 8
STEPS = 2


def dot(left, right):
    return jnp.dot(left, right, preferred_element_type=F32)


def act(values):
    scale = lax.rsqrt(jnp.mean(values * values, axis=-1, keepdims=True) + EPSILON)
    half = values * (scale * 0.5)
    return half + half * jnp.tanh(half)


def shift_on(odd):
    rows = lax.broadcasted_iota(jnp.int32, odd.shape, 0)
    return jnp.where(rows == 0, 0.0, pltpu.roll(odd, 1, 0))


def shift_back(even):
    count = even.shape[0]
    rows = lax.broadcasted_iota(jnp.int32, even.shape, 0)
    return jnp.where(rows == count - 1, 0.0, pltpu.roll(even, count - 1, 0))


def kernel(
    rows_n,
    dims,
    times_ref,
    xin_ref,
    emb_ref,
    win_ref,
    wout_ref,
    stale_hbm,
    wenc_hbm,
    wdown_hbm,
    wtmid_hbm,
    wup_hbm,
    wskip_hbm,
    wdec_hbm,
    wtime_hbm,
    xo_ref,
    feat_ref,
    wenc,
    wdown,
    wtm,
    wup,
    wskip,
    wdec,
    wtime,
    inbuf,
    recvx,
    xs,
    xh,
    lift,
    mixs,
    enc,
    a3e,
    a3d,
    a3g,
    gs,
    gh,
    bs,
    bh,
    lows,
    qs,
    qr,
    taps,
    xcs,
    xch,
    raised,
    mun,
    fsend,
    bias_e,
    bias_m,
    bias_d,
    wsem,
    ssem,
    rsem,
):
    rd, cols, chans, mid = dims
    half = cols // 2
    hr = rd // 2
    seg = lax.axis_index("segment")
    row = lax.axis_index("rows")
    first = seg == 0
    has_up = row > 0
    has_dn = row < rows_n - 1
    up = jnp.maximum(row - 1, 0)
    dn = jnp.minimum(row + 1, rows_n - 1)
    pair = 1 - seg

    fetch = {
        "own": pltpu.make_async_copy(stale_hbm.at[seg], inbuf.at[seg], wsem.at[0]),
        "skip": pltpu.make_async_copy(wskip_hbm, wskip, wsem.at[1]),
        "time": pltpu.make_async_copy(wtime_hbm, wtime, wsem.at[2]),
        "enc": pltpu.make_async_copy(wenc_hbm, wenc, wsem.at[3]),
        "down": pltpu.make_async_copy(wdown_hbm, wdown, wsem.at[4]),
        "dec": pltpu.make_async_copy(wdec_hbm, wdec, wsem.at[5]),
        "tm_own": pltpu.make_async_copy(wtmid_hbm.at[1], wtm.at[0], wsem.at[6]),
        "tm_other": pltpu.make_async_copy(wtmid_hbm.at[2 * pair], wtm.at[1], wsem.at[7]),
        "up": pltpu.make_async_copy(wup_hbm, wup, wsem.at[8]),
    }
    for item in fetch.values():
        item.start()

    def remote(src, dst, index, where):
        return pltpu.make_async_remote_copy(
            src_ref=src,
            dst_ref=dst,
            send_sem=ssem.at[index],
            recv_sem=rsem.at[index],
            device_id=where,
            device_id_type=MESH,
        )

    to_pair, to_up, to_dn = {"segment": pair}, {"rows": up}, {"rows": dn}
    swap = remote(stale_hbm.at[pair], inbuf.at[seg], 0, to_pair)
    swapx = remote(xin_ref.at[pair], recvx, 1, to_pair)
    x_up = remote(xs.at[0], xh.at[1], 2, to_up)
    x_dn = remote(xs.at[rd - 1], xh.at[0], 3, to_dn)
    g_dn = [remote(gs.at[s], gh.at[s], 4 + 6 * s, to_dn) for s in range(STEPS)]
    b_up = [remote(bs.at[s, 0], bh.at[s, 1], 5 + 6 * s, to_up) for s in range(STEPS)]
    b_dn = [remote(bs.at[s, 1], bh.at[s, 0], 6 + 6 * s, to_dn) for s in range(STEPS)]
    q_sw = [remote(qs.at[s], qr.at[s], 7 + 6 * s, to_pair) for s in range(STEPS)]
    c_up = [remote(xcs.at[s, 0], xch.at[s, 1], 8 + 6 * s, to_up) for s in range(STEPS)]
    c_dn = [remote(xcs.at[s, 1], xch.at[s, 0], 9 + 6 * s, to_dn) for s in range(STEPS)]
    f_sw = [
        remote(
            fsend.at[pl.ds(h * hr, hr)],
            feat_ref.at[seg, pl.ds(h * hr, hr)],
            16 + h,
            to_pair,
        )
        for h in range(2)
    ]
    xo_sw = remote(xs, xo_ref.at[seg], 18, to_pair)

    def send_up(copy):
        pl.when(has_up)(copy.start)

    def send_dn(copy):
        pl.when(has_dn)(copy.start)

    barrier = pltpu.get_barrier_semaphore()
    pl.semaphore_signal(barrier, inc=1, device_id=to_pair, device_id_type=MESH)

    @pl.when(has_up)
    def _():
        pl.semaphore_signal(barrier, inc=1, device_id=to_up, device_id_type=MESH)

    @pl.when(has_dn)
    def _():
        pl.semaphore_signal(barrier, inc=1, device_id=to_dn, device_id_type=MESH)

    pl.semaphore_wait(barrier, 1 + has_up.astype(jnp.int32) + has_dn.astype(jnp.int32))
    swap.start()
    swapx.start()

    @pl.when(jnp.logical_not(has_up))
    def _():
        xh[0] = jnp.zeros_like(xh[0])
        for s in range(STEPS):
            gh[s] = jnp.zeros_like(gh[s])
            bh[s, 0] = jnp.zeros_like(bh[s, 0])
            xch[s, 0] = jnp.zeros_like(xch[s, 0])

    @pl.when(jnp.logical_not(has_dn))
    def _():
        xh[1] = jnp.zeros_like(xh[1])
        for s in range(STEPS):
            bh[s, 1] = jnp.zeros_like(bh[s, 1])
            xch[s, 1] = jnp.zeros_like(xch[s, 1])

    def spread(ref, index, values):
        even, odd = values[:half], values[half:]
        even16, odd16 = even.astype(BF16), odd.astype(BF16)
        ref[index, :half, 0:chans] = shift_on(odd).astype(BF16)
        ref[index, half:, 0:chans] = even16
        ref[index, :half, chans : 2 * chans] = even16
        ref[index, half:, chans : 2 * chans] = odd16
        ref[index, :half, 2 * chans :] = odd16
        ref[index, half:, 2 * chans :] = shift_back(even).astype(BF16)

    def spread_down(step, index, values):
        even, odd = values[:half], values[half:]
        a3g[step, index, :, 0:chans] = shift_on(odd).astype(BF16)
        a3g[step, index, :, chans : 2 * chans] = even.astype(BF16)
        a3g[step, index, :, 2 * chans :] = odd.astype(BF16)

    def lift_row(x_row):
        return lax.dot_general(
            x_row.astype(BF16),
            win_ref[...],
            (((0,), (0,)), ((), ())),
            preferred_element_type=F32,
        )

    def enc_front():
        def one(r, carry):
            lifted = lift_row(xs[r])
            lift[r] = lifted
            spread(a3e, r + 1, act(lifted))
            return carry

        lax.fori_loop(0, rd, one, 0)

    def gate_rows(step):
        def one(r, carry):
            g = act(enc[r].astype(F32))
            spread_down(step, r + 1, g)

            @pl.when(r == rd - 1)
            def _():
                gs[step] = g.astype(BF16)

            return carry

        lax.fori_loop(0, rd, one, 0)
        send_dn(g_dn[step])

    def mix_rows(step):
        def one(r, carry):
            if step == 0:
                mixed = dot(inbuf[1, r], wskip[0]) + dot(enc[r], wskip[1])
            else:
                low = dot(raised[r // 2], wskip[0])
                mixed = jnp.concatenate([low, low], axis=0) + dot(enc[r], wskip[1])
            mixs[r] = mixed
            b = act(mixed)
            spread(a3d, r + 1, b)

            @pl.when(r == 0)
            def _():
                bs[step, 0] = b.astype(BF16)

            @pl.when(r == rd - 1)
            def _():
                bs[step, 1] = b.astype(BF16)

            return carry

        lax.fori_loop(0, rd, one, 0)
        send_up(b_up[step])
        send_dn(b_dn[step])

    def conv_half(a3, weight, h):
        total = None
        for dy in range(3):
            window = a3[h * hr + dy : h * hr + dy + hr].reshape(hr * cols, 3 * chans)
            part = dot(window, weight[dy])
            total = part if total is None else total + part
        return total

    def enc_half(step, h):
        base = lift[h * hr : (h + 1) * hr].reshape(hr * cols, chans)
        total = base + conv_half(a3e, wenc, h) + bias_e[step : step + 1]
        return total.astype(BF16).reshape(hr, cols, chans)

    def mid_front(step):
        spread_down(step, 0, gh[step].astype(F32))
        total = None
        for dy in range(3):
            window = jnp.concatenate([a3g[step, dy + 2 * i] for i in range(hr)], axis=0)
            part = dot(window, wdown[dy])
            total = part if total is None else total + part
        low = total + bias_m[step : step + 1]
        lows[...] = low
        qs[step] = act(low).astype(BF16)
        q_sw[step].start()

    def mid_tail(step):
        q_sw[step].wait_recv()
        total = lows[...] + dot(qs[step], wtm[0]) + dot(qr[step], wtm[1])
        lifted = dot(total.astype(BF16), wup[...]).astype(BF16)
        raised[...] = lifted.reshape(hr, half, chans)

    lane = lax.broadcasted_iota(jnp.int32, (SUB, cols), 1)

    def across(left, centre, right):
        before = jnp.where(
            lane < half,
            jnp.where(lane == 0, 0.0, pltpu.roll(left, half + 1, 1)),
            pltpu.roll(left, half, 1),
        )
        after = jnp.where(
            lane < half,
            pltpu.roll(right, half, 1),
            jnp.where(lane == cols - 1, 0.0, pltpu.roll(right, half - 1, 1)),
        )
        return before + centre + after

    def tap(r, k):
        return taps[r, k * SUB : (k + 1) * SUB]

    def coefficient(step):
        return (jnp.full((SUB, cols), times_ref[step]).astype(F32) + 1.0) / 1000.0

    def dec(step):
        pl.when(has_dn)(b_up[step].wait_recv)
        pl.when(has_up)(b_dn[step].wait_recv)
        spread(a3d, 0, bh[step, 0].astype(F32))
        spread(a3d, rd + 1, bh[step, 1].astype(F32))
        for h in range(2):
            base = mixs[h * hr : (h + 1) * hr].reshape(hr * cols, chans)
            total = base + conv_half(a3d, wdec, h) + bias_d[step : step + 1]
            o = act(total).astype(BF16)
            for i in range(hr):
                taps[h * hr + i] = lax.dot_general(
                    wout_ref[...],
                    o[i * cols : (i + 1) * cols],
                    (((1,), (1,)), ((), ())),
                    preferred_element_type=F32,
                )
        coef = coefficient(step)
        for r in range(rd):
            sums = []
            for dx in range(3):
                parts = [tap(r + dy - 1, dy * 3 + dx) for dy in range(3) if 0 <= r + dy - 1 < rd]
                sums.append(functools.reduce(jnp.add, parts))
            xs[r] = xs[r] - coef * across(*sums)
        xcs[step, 0, 0] = xs[0]
        xcs[step, 0, 1] = coef * across(tap(0, 6), tap(0, 7), tap(0, 8))
        xcs[step, 1, 0] = xs[rd - 1]
        xcs[step, 1, 1] = coef * across(tap(rd - 1, 0), tap(rd - 1, 1), tap(rd - 1, 2))
        send_up(c_up[step])
        send_dn(c_dn[step])

    def finish_x(step):
        pl.when(has_dn)(c_up[step].wait_recv)
        pl.when(has_up)(c_dn[step].wait_recv)
        xs[0] = xs[0] - xch[step, 0, 1]
        xs[rd - 1] = xs[rd - 1] - xch[step, 1, 1]

    swapx.wait_recv()
    xs[...] = xin_ref[seg] + recvx[...]
    send_up(x_up)
    send_dn(x_dn)
    enc_front()

    at = lax.broadcasted_iota(jnp.int32, (cols, cols), 0)
    col = lax.broadcasted_iota(jnp.int32, (cols, cols), 1)
    source = jnp.where(at < half, 2 * at, 2 * (at - half) + 1)
    sort = jnp.where(col == source, 1.0, 0.0).astype(BF16)
    fetch["own"].wait()
    swap.wait_recv()

    def arrange(r, carry):
        enc[r] = dot(sort, inbuf[0, r]).astype(BF16)
        inbuf[1, r] = dot(sort, inbuf[1, r]).astype(BF16)
        return carry

    lax.fori_loop(0, rd, arrange, 0)
    gate_rows(0)
    fetch["skip"].wait()
    mix_rows(0)

    fetch["time"].wait()
    bias = dot(emb_ref[...], wtime[...])
    bias_e[...] = bias[:, :chans]
    bias_m[...] = bias[:, chans : chans + mid]
    bias_d[...] = bias[:, chans + mid :]

    pl.when(has_dn)(x_up.wait_recv)
    pl.when(has_up)(x_dn.wait_recv)
    spread(a3e, 0, act(lift_row(xh[0])))
    spread(a3e, rd + 1, act(lift_row(xh[1])))
    pl.when(has_up)(x_up.wait_send)
    pl.when(has_dn)(x_dn.wait_send)
    fetch["enc"].wait()
    for h in range(2):
        enc[h * hr : (h + 1) * hr] = enc_half(0, h)
    gate_rows(1)
    fetch["down"].wait()
    pl.when(has_up)(g_dn[0].wait_recv)
    mid_front(0)
    fetch["dec"].wait()
    dec(0)
    fetch["tm_own"].wait()
    fetch["tm_other"].wait()
    fetch["up"].wait()
    mid_tail(0)

    mix_rows(1)
    pl.when(has_up)(g_dn[1].wait_recv)
    mid_front(1)
    finish_x(0)
    enc_front()
    above = xch[0, 0, 0] - xcs[0, 0, 1]
    below = xch[0, 1, 0] - xcs[0, 1, 1]
    above = above * jnp.full(above.shape, has_up.astype(jnp.int32)).astype(F32)
    below = below * jnp.full(below.shape, has_dn.astype(jnp.int32)).astype(F32)
    spread(a3e, 0, act(lift_row(above)))
    spread(a3e, rd + 1, act(lift_row(below)))
    dec(1)
    mid_tail(1)

    at2 = lax.broadcasted_iota(jnp.int32, (cols, half), 0)
    col2 = lax.broadcasted_iota(jnp.int32, (cols, half), 1)
    twice = jnp.where(col2 == at2 // 2, 1.0, 0.0).astype(BF16)
    target = jnp.where(col < half, 2 * col, 2 * (col - half) + 1)
    unsort = jnp.where(at == target, 1.0, 0.0).astype(BF16)
    for i in range(hr):
        wide = dot(twice, raised[i]).astype(BF16)
        mun[2 * i] = wide
        mun[2 * i + 1] = wide
    for h in range(2):
        fresh = enc_half(1, h)
        plain = [dot(unsort, fresh[i]).astype(BF16) for i in range(hr)]

        @pl.when(first)
        def _():
            for i in range(hr):
                feat_ref[0, h * hr + i] = plain[i]
                fsend[h * hr + i] = mun[h * hr + i]

        @pl.when(jnp.logical_not(first))
        def _():
            for i in range(hr):
                feat_ref[1, h * hr + i] = mun[h * hr + i]
                fsend[h * hr + i] = plain[i]

        f_sw[h].start()
        if h == 0:
            finish_x(1)
            xo_ref[seg] = xs[...]
            xo_sw.start()

    swap.wait_send()
    swapx.wait_send()
    for s in range(STEPS):
        pl.when(has_dn)(g_dn[s].wait_send)
        pl.when(has_up)(b_up[s].wait_send)
        pl.when(has_dn)(b_dn[s].wait_send)
        q_sw[s].wait_send()
        pl.when(has_up)(c_up[s].wait_send)
        pl.when(has_dn)(c_dn[s].wait_send)
    for copy in (*f_sw, xo_sw):
        copy.wait()


def body(rows_n, latent, stale, timesteps, w_in, w_enc, w_down, w_tmid, w_up, w_skip, w_dec, w_out, w_time):
    frames, rd, merged = latent.shape
    cols, chans = stale.shape[3], stale.shape[4]
    mid = w_down.shape[3]
    lat = w_in.shape[0]
    segs = cols * lat // merged
    half, hr = cols // 2, rd // 2
    part = half // segs
    seg = lax.axis_index("segment")

    pieces = latent.reshape(frames, rd, part, 2, lat).transpose(0, 1, 4, 3, 2)
    mine = (jnp.arange(segs) == seg)[None, None, None, None, :, None]
    xin = jnp.where(mine, pieces[:, :, :, :, None, :], 0.0).reshape(frames, rd, lat, cols)
    xin = jnp.pad(xin, ((0, 0), (0, 0), (0, SUB - lat), (0, 0)))

    quarter = w_time.shape[0] // 2
    freqs = jnp.exp(-math.log(10000.0) * jnp.arange(quarter).astype(F32) / quarter)
    angles = timesteps.astype(F32)[:, None] * freqs
    emb = jax.nn.silu(jnp.concatenate([jnp.sin(angles), jnp.cos(angles)], axis=1)).astype(BF16)
    emb = jnp.pad(emb, ((0, 16 - emb.shape[0]), (0, 0)))

    win = jnp.pad(w_in, ((0, SUB - lat), (0, 0)))
    wout = jnp.pad(w_out.transpose(0, 1, 3, 2), ((0, 0), (0, 0), (0, SUB - lat), (0, 0)))
    wout = wout.reshape(9 * SUB, chans)

    vmem = pl.BlockSpec(memory_space=pltpu.VMEM)
    anywhere = pl.BlockSpec(memory_space=pl.ANY)
    rowed = (rd, cols, chans)
    xo, feat = pl.pallas_call(
        functools.partial(kernel, rows_n, (rd, cols, chans, mid)),
        out_shape=(
            jax.ShapeDtypeStruct((frames, rd, SUB, cols), F32),
            jax.ShapeDtypeStruct((frames, *rowed), BF16),
        ),
        in_specs=[pl.BlockSpec(memory_space=pltpu.SMEM)] + [vmem] * 4 + [anywhere] * 8,
        out_specs=(vmem, vmem),
        scratch_shapes=[
            pltpu.VMEM((3, 3 * chans, chans), BF16),
            pltpu.VMEM((3, 3 * chans, mid), BF16),
            pltpu.VMEM((2, mid, mid), BF16),
            pltpu.VMEM((mid, chans), BF16),
            pltpu.VMEM((2, chans, chans), BF16),
            pltpu.VMEM((3, 3 * chans, chans), BF16),
            pltpu.VMEM(w_time.shape, BF16),
            pltpu.VMEM((2, *rowed), BF16),
            pltpu.VMEM((rd, SUB, cols), F32),
            pltpu.VMEM((rd, SUB, cols), F32),
            pltpu.VMEM((2, SUB, cols), F32),
            pltpu.VMEM(rowed, F32),
            pltpu.VMEM(rowed, F32),
            pltpu.VMEM(rowed, BF16),
            pltpu.VMEM((rd + 2, cols, 3 * chans), BF16),
            pltpu.VMEM((rd + 2, cols, 3 * chans), BF16),
            pltpu.VMEM((STEPS, rd + 1, half, 3 * chans), BF16),
            pltpu.VMEM((STEPS, cols, chans), BF16),
            pltpu.VMEM((STEPS, cols, chans), BF16),
            pltpu.VMEM((STEPS, 2, cols, chans), BF16),
            pltpu.VMEM((STEPS, 2, cols, chans), BF16),
            pltpu.VMEM((hr * half, mid), F32),
            pltpu.VMEM((STEPS, hr * half, mid), BF16),
            pltpu.VMEM((STEPS, hr * half, mid), BF16),
            pltpu.VMEM((rd, 9 * SUB, cols), F32),
            pltpu.VMEM((STEPS, 2, 2, SUB, cols), F32),
            pltpu.VMEM((STEPS, 2, 2, SUB, cols), F32),
            pltpu.VMEM((hr, half, chans), BF16),
            pltpu.VMEM(rowed, BF16),
            pltpu.VMEM(rowed, BF16),
            pltpu.VMEM((16, chans), F32),
            pltpu.VMEM((16, mid), F32),
            pltpu.VMEM((16, chans), F32),
            pltpu.SemaphoreType.DMA((9,)),
            pltpu.SemaphoreType.DMA((19,)),
            pltpu.SemaphoreType.DMA((19,)),
        ],
        compiler_params=pltpu.CompilerParams(
            collective_id=0, has_side_effects=True, vmem_limit_bytes=56 * 2**20
        ),
    )(
        timesteps,
        xin,
        emb,
        win,
        wout,
        stale[0],
        w_enc.reshape(3, 3 * chans, chans),
        w_down.reshape(3, 3 * chans, mid),
        w_tmid,
        w_up,
        w_skip.reshape(2, chans, chans),
        w_dec.reshape(3, 3 * chans, chans),
        w_time,
    )
    whole = xo[:, :, :lat].reshape(frames, rd, lat, 2, segs, part)
    own = lax.dynamic_index_in_dim(whole, seg, axis=4, keepdims=False)
    result = own.transpose(0, 1, 4, 3, 2).reshape(frames, rd, merged)
    return (result, feat[None])


def solution(mesh):
    placed = (
        P("clips", "rows", "segment"),
        P("segment", "clips", "rows", None, None),
        P("clips"),
        P(),
        P(),
        P(),
        P(),
        P(),
        P(),
        P(),
        P(),
        P(),
    )
    return jax.shard_map(
        functools.partial(body, mesh.shape["rows"]),
        mesh=mesh,
        in_specs=placed,
        out_specs=(P("clips", "rows", "segment"), P("segment", "clips", "rows", None, None)),
        check_vma=False,
    )
```

time: 250 us -> 58.9 us (0.24); the launches traced: 245 us -> 58.1 us
  matrix products: 86.9 us -> 0 us
  starting transfers between devices: 48.5 us -> 0 us
  Pallas kernels: 0 us -> 41.5 us
  local copies, waits for them, and re-layouts: 52.4 us -> 14.9 us
  waiting for transfers between devices: 29.2 us -> 0 us
  other arithmetic: 14.8 us -> 0.98 us
  loops' own time: 8.88 us -> 0 us
    dot_general x60 -> x0, matrix products: 86.9 us -> none  [the longest x54 78.8 us: conv_rows(): jnp.einsum('fhwc,co->fhwo', window, weight[row_off, col_off], preferred_e...]
    ppermute x15 -> x0, starting transfers between devices: 48.5 us -> none  [the longest x6 27.5 us: with_halo(): before = lax.ppermute(last, axis, up)]
    another operation x15 -> x0, local copies, waits for them, and re-layouts: 41.7 us -> none
    pallas_call x0 -> x1, Pallas kernels: none -> 41.5 us  [body(): pl.pallas_call(functools.partial(kernel, rows_n, (rd, cols, chans, mid)),...]
    ppermute x15 -> x0, waiting for transfers between devices: 29.2 us -> none  [the longest x6 22.3 us: with_halo(): after = lax.ppermute(first, axis, down)]
    another operation x4 -> x0, loops' own time: 8.64 us -> none  [the longest x2 7.9 us: body(): lax.cond(first, enc_middle, mid_middle, (spread, lifted, state, other))]
    unnamed x14 -> x8, local copies, waits for them, and re-layouts: 0.04 us -> 6.73 us
    concatenate x6 -> x0, other arithmetic: 6.62 us -> none  [with_halo(): value = jnp.concatenate([before, value, after], axis=dim)]
  transfers between devices with their start and end apart: 15 -> 0, of which waited for: 11 -> 0; matrix products, arithmetic and copies ran while one was open for 17% -> 0% of each run, Pallas kernels for 0% -> 0%
where the time goes in v1:
time: 58.9 us; the launch traced here: 58.1 us
  Pallas kernels  41.5 us (70%)
  local copies, waits for them, and re-layouts  14.9 us (25%)
  other arithmetic  0.98 us (2%)
  between operations  0.72 us (1%)
    pallas_call x1, Pallas kernels, body(): pl.pallas_call(functools.partial(kernel, rows_n, (rd, cols, chans, mid)),...  41.5 us
    unnamed x8, local copies, waits for them, and re-layouts  6.73 us
    pad x1, local copies, waits for them, and re-layouts, body(): jnp.pad(w_out.transpose(0, 1, 3, 2), ((0, 0), (0, 0), (0, SUB - lat), (0,...  1.37 us
    reshape x1, local copies, waits for them, and re-layouts, body(): pieces = latent.reshape(frames, rd, part, 2, lat).transpose(0, 1, 4, 3, 2)  1.31 us
    pad x1, local copies, waits for them, and re-layouts, body(): win = jnp.pad(w_in, ((0, SUB - lat), (0, 0)))  1.3 us

profile of v1, /device:TPU:0, one launch (start us, length us, event | category | flops | bytes accessed | tf_op | source)
XLA Modules:
  0.0 58.1 jit_solution(4802924470061195377)
XLA Ops:
  0.6 0.0 copy-start.1
  0.7 0.1 broadcast_in_dim.33
  0.7 0.1 broadcast_in_dim.34
  0.8 0.8 %convert_element_type.21 = f32[2]{0:T(128)S(1)} convert(s32[2]{0:T(128)} %times_ref.1) | non-fusion elementwise | flops 2 | bytes 16 | tf_op jit(solution)/shard_map/convert_element_type | solution.py:473
  1.6 0.1 multiply_sine_fusion
  1.7 0.1 fusion
  1.8 1.3 %pad.18.win_ref = bf16[8,320]{1,0:T(8,128)(2,1)} pad(bf16[4,320]{1,0:T(4,128)(2,1)} %param.15, bf16[]{:T(256)} %constant.23.clone.1), padding=0_4x0_0 | pad | bytes 7682 | tf_op jit(solution)/shard_map/jit(_pad)/pad | solution.py:477
  3.1 0.6 %pad.17.emb_ref = bf16[16,320]{1,0:T(8,128)(2,1)} pad(bf16[2,320]{1,0:T(2,128)(2,1)S(1)} %fusion, bf16[]{:T(256)} %constant.23.clone.1), padding=0_14x0_0 | pad | bytes 11522 | tf_op jit(solution)/shard_map/jit(_pad)/pad | solution.py:475
  3.7 1.4 %pad.19 = bf16[3,3,8,320]{3,2,1,0:T(8,128)(2,1)} pad(bf16[3,3,4,320]{3,2,1,0:T(4,128)(2,1)} %bitcast.27, bf16[]{:T(256)} %constant.23.clone.1), padding=0_0x0_0x0_4x0_0 | pad | bytes 69122 | tf_op jit(solution)/shard_map/jit(_pad)/pad | solution.py:478
  5.1 1.3 %reshape.43 = f32[2,6,32,2,4]{4,3,2,0,1:T(2,128)S(1)} reshape(f32[2,6,256]{2,0,1:T(2,128)} %param.12) | data formatting | bytes 24576 | tf_op jit(solution)/shard_map/reshape | solution.py:466
  6.4 0.2 copy.19
  6.6 0.1 broadcast_in_dim.36
  6.7 0.1 broadcast_in_dim.37
  6.8 0.6 %pad.16.xin_ref = f32[2,6,8,128]{3,2,1,0:T(8,128)} pad(f32[2,6,4,128]{3,2,1,0:T(4,128)S(1)} %broadcast_select_fusion, f32[]{:T(128)} %constant.20.clone.1), padding=0_0x0_0x0_4x0_0 | pad | bytes 73732 | tf_op jit(solution)/shard_map/jit(_pad)/pad | solution.py:469
  7.4 2.0 %copy.22.wup_hbm = bf16[640,320]{1,0:T(8,128)(2,1)} copy(bf16[640,320]{0,1:T(8,128)(2,1)} %param.19) | data formatting | bytes 819200 | tf_op args[7]
  9.4 1.0 %copy.21 = bf16[640,320]{1,0:T(8,128)(2,1)} copy(bf16[640,320]{0,1:T(8,128)(2,1)S(1)} %copy-done.1) | data formatting | bytes 819200 | tf_op args[8]
  10.4 1.4 %copy.20 = bf16[1,2,6,128,320]{4,3,2,1,0:T(8,128)(2,1)} copy(bf16[1,2,6,128,320]{3,4,2,1,0:T(8,128)(2,1)S(1)} %copy-done) | data formatting | bytes 1966080 | tf_op args[1]
  11.8 41.5 %shard_map.131 = (f32[2,6,8,128]{3,2,1,0:T(8,128)}, bf16[2,6,128,320]{3,2,1,0:T(8,128)(2,1)}) custom-call(s32[2]{0:T(128)} %times_ref.1, f32[2,6,8,128]{3,2,1,0:T(8,128)} %pad.16.xin_ref, bf16[16,320]{1,0:T(8,128)(2,1)} %pad.17.emb_ref, bf16[8,320]{1,0:T(8,128)(2,1)} %pad.18.win_ref, bf16[72,320]{1,0:T(8,128)(2,1)} %bitcast.25, ...), custom_call_target="tpu_custom_call" | custom-call | tf_op jit(solution)/shard_map/pallas_call | solution.py:484
  53.4 0.8 %slice.3 = f32[2,6,4,128]{3,2,1,0:T(4,128)S(1)} slice(f32[2,6,8,128]{3,2,1,0:T(8,128)} %get-tuple-element.4), slice={[0:2], [0:6], [0:4], [0:128]} | slice | bytes 49152 | tf_op jit(solution)/shard_map/slice | solution.py:548
  54.2 2.3 %copy.25 = bf16[1,2,6,128,320]{3,4,2,1,0:T(8,128)(2,1)} copy(bf16[1,2,6,128,320]{4,3,2,1,0:T(8,128)(2,1)} %bitcast.24) | data formatting | bytes 1966080
  56.5 0.1 reshape.49
  56.6 0.1 constant_dynamic-slice_fusion
  56.7 0.3 copy.24
  57.0 1.1 %reshape.50 = f32[2,6,256]{2,0,1:T(2,128)} reshape(f32[2,6,32,2,4]{4,3,2,0,1:T(2,128)S(1)} %copy.24) | data formatting | bytes 24576 | tf_op jit(solution)/shard_map/reshape | solution.py:550
  (6 shorter events, 0.0 us)
Async XLA Ops:
  0.6 8.8 %copy-start.1 = (bf16[640,320]{0,1:T(8,128)(2,1)S(1)}, bf16[640,320]{0,1:T(8,128)(2,1)}, u32[]{:S(2)}) copy-start(bf16[640,320]{0,1:T(8,128)(2,1)} %param.20) | copy-start | bytes 1228804
  0.6 9.8 %copy-start = (bf16[1,2,6,128,320]{3,4,2,1,0:T(8,128)(2,1)S(1)}, bf16[1,2,6,128,320]{3,4,2,1,0:T(8,128)(2,1)}, u32[]{:S(2)}) copy-start(bf16[1,2,6,128,320]{3,4,2,1,0:T(8,128)(2,1)} %param.13) | copy-start | bytes 2949124
